TPU v7x, 32 devices: a whole 2x2x4 slice. The times are simulated.
32 devices in a mesh: row: 8 (over z, y), col: 4 (over x, core).
Axes of the slice: x: 2, y: 2, z: 4, core: 2. Of those that a mesh axis runs over, the one named last changes fastest.
Arguments:
- integrals: float32 [2048, 20480], P('row', 'col'), may hold values from -6 to 6
- factor: float32 [2048, 2048], P('row', 'col'), may hold values from -1 to 2, as said below
Outputs:
- coefficients: float32 [2048, 20480], P('row', 'col')
Inputs may be any that keep to these rules, and one draw needn't show every extreme that they name: factor is zero above its diagonal (column index greater than row index) and between 1 and 2 on it.
All inputs are finite; a program needn't handle non-finite values.
Results may differ from a plain program's by a relative error of at most 0.0001.
Values sent between devices are 32-bit elements; how exact they have to be, the bound alone decides.
A program may use at most 64 MiB of HBM per device.

v0:
```python
import jax
import jax.numpy as jnp
from jax import lax
from jax.sharding import PartitionSpec as P

PANEL = 256
PANELS = 8


def spread(value, axis, source):
    kept = jnp.where(lax.axis_index(axis) == source, value, 0).astype(value.dtype)
    return lax.psum(kept, axis)


def local_solve(current, factor_block, span, owner, my_row):
    lower_block = jnp.where(my_row == owner, factor_block, jnp.eye(span, dtype=jnp.float32))
    return jax.scipy.linalg.solve_triangular(lower_block, current, lower=True)


def apply_panel(current, factor_block, solved, start, span, owner, my_row, global_rows):
    rows_here = current.shape[0]
    product = jnp.dot(
        factor_block, solved, precision=lax.Precision.HIGHEST, preferred_element_type=jnp.float32
    )
    below_panel = global_rows >= start + span
    updated = jnp.where(below_panel[:, None], current - product, current)
    local_start = start - owner * rows_here
    placed = updated.at[local_start : local_start + span].set(solved)
    return jnp.where(my_row == owner, placed, updated)


def shards(integrals, factor):
    rows_here = integrals.shape[0]
    my_row = lax.axis_index("row")
    global_rows = my_row * rows_here + jnp.arange(rows_here, dtype=jnp.int32)
    current = integrals
    whole_factor = lax.all_gather(factor, "col", axis=1, tiled=True)
    for panel_index in range(PANELS):
        start = panel_index * PANEL
        owner = start // rows_here
        factor_block = whole_factor[:, start : start + PANEL]
        solved = spread(local_solve(current, factor_block, PANEL, owner, my_row), "row", owner)
        current = apply_panel(
            current, factor_block, solved, start, PANEL, owner, my_row, global_rows
        )
    return current


def solution(mesh):
    placed = (P("row", "col"), P("row", "col"))
    return jax.shard_map(
        shards, mesh=mesh, in_specs=placed, out_specs=P("row", "col"), check_vma=False
    )
```

profile of v0, /device:TPU:28, one launch (start us, length us, event | category | flops | bytes accessed | tf_op | source)
XLA Modules:
  0.0 1719.4 jit_solution(12105040731372619840)
XLA Ops:
  7.3 25.1 %all-gather.2.cloned.1.call-done = f32[256,2048]{1,0:T(8,128)} async-done(((f32[256,512]{1,0:T(8,128)}), f32[256,2048]{1,0:T(8,128)}) %all-gather.2.cloned.1.call-update) | async-done | bytes 2097168 | tf_op jit(solution)/shard_map/all_gather | solution.py:37
  32.5 2.5 fusion.24
  35.1 4.2 while.32
  39.3 19.7 %custom-call.10 = f32[2,128,128]{1,2,0:T(8,128)S(1)} custom-call(f32[2,128,128]{2,1,0:T(8,128)S(1)} %get-tuple-element.216), custom_call_target="InvertDiagBlocksLowerTriangular" | custom-call | tf_op jit(solution)/shard_map/jit(_solve_triangular)/triangular_solve | solution.py:17
  59.0 4.3 fusion.22
  68.2 2.9 maximum_select_fusion
  71.7 5.9 while.33
  77.7 20.3 %custom-call.11 = f32[2,128,128]{1,2,0:T(8,128)} custom-call(f32[2,128,128]{2,1,0:T(8,128)S(1)} %get-tuple-element.217), custom_call_target="InvertDiagBlocksLowerTriangular" | custom-call | tf_op jit(solution)/shard_map/jit(_solve_triangular)/triangular_solve | solution.py:17
  98.0 155.2 %all-reduce.9.cloned.1.call-done = f32[256,5120]{1,0:T(8,128)} async-done(((f32[256,5120]{1,0:T(8,128)}), f32[256,5120]{1,0:T(8,128)}) %all-reduce.9.cloned.1.call-update) | async-done | bytes 5242896 | tf_op jit(solution)/shard_map/psum | solution.py:12
  253.1 12.7 fusion.7
  268.3 3.3 convolution_subtract_fusion.6
  274.1 2.9 maximum_select_fusion.1
  277.2 6.1 while.34
  283.3 20.3 %custom-call.12 = f32[2,128,128]{1,2,0:T(8,128)} custom-call(f32[2,128,128]{2,1,0:T(8,128)S(1)} %get-tuple-element.218), custom_call_target="InvertDiagBlocksLowerTriangular" | custom-call | tf_op jit(solution)/shard_map/jit(_solve_triangular)/triangular_solve | solution.py:17
  303.6 156.7 %all-reduce.11.cloned.1.call-done = f32[256,5120]{1,0:T(8,128)} async-done(((f32[256,5120]{1,0:T(8,128)}), f32[256,5120]{1,0:T(8,128)}) %all-reduce.11.cloned.1.call-update) | async-done | bytes 5242896 | tf_op jit(solution)/shard_map/psum | solution.py:12
  460.3 12.8 fusion.6
  475.6 3.3 convolution_subtract_fusion.5
  481.5 2.9 maximum_select_fusion.2
  484.5 4.3 while.35
  488.8 20.3 %custom-call.13 = f32[2,128,128]{1,2,0:T(8,128)} custom-call(f32[2,128,128]{2,1,0:T(8,128)S(1)} %get-tuple-element.219), custom_call_target="InvertDiagBlocksLowerTriangular" | custom-call | tf_op jit(solution)/shard_map/jit(_solve_triangular)/triangular_solve | solution.py:17
  509.1 158.5 %all-reduce.13.cloned.1.call-done = f32[256,5120]{1,0:T(8,128)} async-done(((f32[256,5120]{1,0:T(8,128)}), f32[256,5120]{1,0:T(8,128)}) %all-reduce.13.cloned.1.call-update) | async-done | bytes 5242896 | tf_op jit(solution)/shard_map/psum | solution.py:12
  667.6 13.1 fusion.5
  683.2 2.5 convolution_subtract_fusion.4
  688.2 2.9 maximum_select_fusion.3
  691.2 4.2 while.36
  695.4 19.7 %custom-call.14 = f32[2,128,128]{1,2,0:T(8,128)S(1)} custom-call(f32[2,128,128]{2,1,0:T(8,128)S(1)} %get-tuple-element.220), custom_call_target="InvertDiagBlocksLowerTriangular" | custom-call | tf_op jit(solution)/shard_map/jit(_solve_triangular)/triangular_solve | solution.py:17
  715.1 159.3 %all-reduce.15.cloned.1.call-done = f32[256,5120]{1,0:T(8,128)} async-done(((f32[256,5120]{1,0:T(8,128)}), f32[256,5120]{1,0:T(8,128)}) %all-reduce.15.cloned.1.call-update) | async-done | bytes 5242896 | tf_op jit(solution)/shard_map/psum | solution.py:12
  874.4 12.6 fusion.4
  894.5 2.9 maximum_select_fusion.4
  897.5 4.3 while.37
  901.8 19.7 %custom-call.15 = f32[2,128,128]{1,2,0:T(8,128)S(1)} custom-call(f32[2,128,128]{2,1,0:T(8,128)S(1)} %get-tuple-element.221), custom_call_target="InvertDiagBlocksLowerTriangular" | custom-call | tf_op jit(solution)/shard_map/jit(_solve_triangular)/triangular_solve | solution.py:17
  921.5 159.2 %all-reduce.17.cloned.1.call-done = f32[256,5120]{1,0:T(8,128)} async-done(((f32[256,5120]{1,0:T(8,128)}), f32[256,5120]{1,0:T(8,128)}) %all-reduce.17.cloned.1.call-update) | async-done | bytes 5242896 | tf_op jit(solution)/shard_map/psum | solution.py:12
  1080.6 12.6 fusion.3
  1095.8 2.5 convolution_subtract_fusion.2
  1100.8 2.9 maximum_select_fusion.5
  1103.8 4.6 while.38
  1108.3 19.7 %custom-call.16 = f32[2,128,128]{1,2,0:T(8,128)S(1)} custom-call(f32[2,128,128]{2,1,0:T(8,128)S(1)} %get-tuple-element.222), custom_call_target="InvertDiagBlocksLowerTriangular" | custom-call | tf_op jit(solution)/shard_map/jit(_solve_triangular)/triangular_solve | solution.py:17
  1128.0 158.8 %all-reduce.19.cloned.1.call-done = f32[256,5120]{1,0:T(8,128)} async-done(((f32[256,5120]{1,0:T(8,128)}), f32[256,5120]{1,0:T(8,128)}) %all-reduce.19.cloned.1.call-update) | async-done | bytes 5242896 | tf_op jit(solution)/shard_map/psum | solution.py:12
  1286.8 12.5 fusion.2
  1301.9 2.5 convolution_subtract_fusion.1
  1306.9 2.9 maximum_select_fusion.6
  1309.9 4.2 while.39
  1314.1 19.7 %custom-call.17 = f32[2,128,128]{1,2,0:T(8,128)S(1)} custom-call(f32[2,128,128]{2,1,0:T(8,128)S(1)} %get-tuple-element.223), custom_call_target="InvertDiagBlocksLowerTriangular" | custom-call | tf_op jit(solution)/shard_map/jit(_solve_triangular)/triangular_solve | solution.py:17
  1333.8 159.2 %all-reduce.21.cloned.1.call-done = f32[256,5120]{1,0:T(8,128)} async-done(((f32[256,5120]{1,0:T(8,128)}), f32[256,5120]{1,0:T(8,128)}) %all-reduce.21.cloned.1.call-update) | async-done | bytes 5242896 | tf_op jit(solution)/shard_map/psum | solution.py:12
  1493.0 12.6 fusion.1
  1513.0 2.9 maximum_select_fusion.7
  1516.0 183.2 %all-reduce.23.cloned.1.call-done = f32[256,5120]{1,0:T(8,128)} async-done(((f32[256,5120]{1,0:T(8,128)}), f32[256,5120]{1,0:T(8,128)}) %all-reduce.23.cloned.1.call-update) | async-done | bytes 5242896 | tf_op jit(solution)/shard_map/psum | solution.py:12
  1699.2 13.5 fusion
  (126 shorter events, 82.0 us)
Async XLA Ops:
  6.5 25.9 %all-gather.2.cloned.1.call-start = ((), (), s32[]{:S(2)}) async-start(), calls=%async_computation | async-start | bytes 2621440 | tf_op jit(solution)/shard_map/all_gather | solution.py:37
  7.3 245.9 %all-reduce.9.cloned.1.call-start = ((), (), s32[]{:S(2)}) async-start(), calls=%async_computation.1 | async-start | bytes 10485760 | tf_op jit(solution)/shard_map/psum | solution.py:12
  58.9 4.3 copy-start.7
  71.1 182.0 %copy-start.8 = (f32[256,2048]{1,0:T(8,128)S(1)}, f32[256,2048]{1,0:T(8,128)}, u32[]{:S(2)}) copy-start(f32[256,2048]{1,0:T(8,128)} %all-gather.2.cloned.1.call-done) | copy-start | bytes 6291460
  71.1 389.2 %all-reduce.11.cloned.1.call-start = ((), (), s32[]{:S(2)}) async-start(), calls=%async_computation.2 | async-start | bytes 10485760 | tf_op jit(solution)/shard_map/psum | solution.py:12
  97.9 167.9 %copy-start.11 = (f32[2,128,128]{1,2,0:T(8,128)S(1)}, f32[2,128,128]{1,2,0:T(8,128)}, u32[]{:S(2)}) copy-start(f32[2,128,128]{1,2,0:T(8,128)} %custom-call.11) | copy-start | bytes 393220
  265.8 2.5 copy-start.5
  277.1 390.5 %all-reduce.13.cloned.1.call-start = ((), (), s32[]{:S(2)}) async-start(), calls=%async_computation.3 | async-start | bytes 10485760 | tf_op jit(solution)/shard_map/psum | solution.py:12
  303.6 169.6 %copy-start.9 = (f32[2,128,128]{1,2,0:T(8,128)S(1)}, f32[2,128,128]{1,2,0:T(8,128)}, u32[]{:S(2)}) copy-start(f32[2,128,128]{1,2,0:T(8,128)} %custom-call.12) | copy-start | bytes 393220
  473.2 2.5 copy-start.1
  484.4 390.0 %all-reduce.15.cloned.1.call-start = ((), (), s32[]{:S(2)}) async-start(), calls=%async_computation.4 | async-start | bytes 10485760 | tf_op jit(solution)/shard_map/psum | solution.py:12
  509.1 171.6 %copy-start.10 = (f32[2,128,128]{1,2,0:T(8,128)S(1)}, f32[2,128,128]{1,2,0:T(8,128)}, u32[]{:S(2)}) copy-start(f32[2,128,128]{1,2,0:T(8,128)} %custom-call.13) | copy-start | bytes 393220
  680.7 2.5 copy-start.2
  691.1 389.5 %all-reduce.17.cloned.1.call-start = ((), (), s32[]{:S(2)}) async-start(), calls=%async_computation.5 | async-start | bytes 10485760 | tf_op jit(solution)/shard_map/psum | solution.py:12
  887.0 2.5 copy-start.3
  897.4 389.4 %all-reduce.19.cloned.1.call-start = ((), (), s32[]{:S(2)}) async-start(), calls=%async_computation.6 | async-start | bytes 10485760 | tf_op jit(solution)/shard_map/psum | solution.py:12
  1093.3 2.5 copy-start.4
  1103.7 389.3 %all-reduce.21.cloned.1.call-start = ((), (), s32[]{:S(2)}) async-start(), calls=%async_computation.7 | async-start | bytes 10485760 | tf_op jit(solution)/shard_map/psum | solution.py:12
  1299.4 2.5 copy-start
  1309.8 389.4 %all-reduce.23.cloned.1.call-start = ((), (), s32[]{:S(2)}) async-start(), calls=%async_computation.8 | async-start | bytes 10485760 | tf_op jit(solution)/shard_map/psum | solution.py:12
  1505.6 2.5 copy-start.6
Sparse Core Ops, SparseCore 0:
  8.9 23.5 all-gather.1
  71.2 181.8 all-reduce.8
  277.2 183.0 all-reduce.10
  484.5 183.0 all-reduce.12
  691.2 183.1 all-reduce.14
  897.5 183.0 all-reduce.16
  1103.8 182.9 all-reduce.18
  1309.9 182.9 all-reduce.20
  1516.1 183.0 all-reduce.22
where the time goes:
time: 1730 us; the launch traced here: 1720 us
  waiting for transfers between devices  1320 us (76%)
  other arithmetic  185 us (11%)
  matrix products  165 us (10%)
  local copies, waits for them, and re-layouts  36 us (2%)
    psum x8, waiting for transfers between devices, spread(): return lax.psum(kept, axis)  1290 us
    another operation x10, other arithmetic, local_solve(): return jax.scipy.linalg.solve_triangular(lower_block, current, lower=True)  162 us
    dot_general x8, matrix products, apply_panel(): jnp.dot(factor_block, solved, precision=lax.Precision.HIGHEST, preferred_...  102 us
    another operation x24, matrix products, local_solve(): return jax.scipy.linalg.solve_triangular(lower_block, current, lower=True)  62.8 us
    another operation x57, local copies, waits for them, and re-layouts, local_solve(): return jax.scipy.linalg.solve_triangular(lower_block, current, lower=True)  35.9 us
  transfers between devices with their start and end apart: 9, of which 9 were waited for; matrix products, arithmetic and copies ran while one was open for 10% of the time, Pallas kernels for 0%

commit v1 on v0

v1 whole, which is shorter than its diff:
```python
import functools

import jax
import jax.numpy as jnp
from jax import lax
from jax.experimental import pallas as pl
from jax.experimental.pallas import tpu as pltpu
from jax.sharding import PartitionSpec as P

MESH = pl.DeviceIdType.MESH
SUB = 128
LANES = 128


def split(value):
    high = value.astype(jnp.bfloat16)
    return high, (value - high.astype(jnp.float32)).astype(jnp.bfloat16)


def dot3(left, right_high, right_low):
    left_high, left_low = split(left)
    mm = functools.partial(jnp.dot, preferred_element_type=jnp.float32)
    return mm(left_high, right_high) + (mm(left_high, right_low) + mm(left_low, right_high))


def invert_lower(block):
    size = block.shape[0]
    mm = functools.partial(
        jnp.dot, precision=lax.Precision.HIGHEST, preferred_element_type=jnp.float32
    )
    rows = lax.broadcasted_iota(jnp.int32, (size, size), 0)
    cols = lax.broadcasted_iota(jnp.int32, (size, size), 1)
    inverse = jnp.where(rows == cols, 1.0 / jnp.where(rows == cols, block, 1.0), 0.0)
    span = 1
    while span < size:
        pair = (rows // (2 * span) == cols // (2 * span)) & (rows // span > cols // span)
        below = jnp.where(pair, block, 0.0)
        inverse = inverse - mm(inverse, mm(below, inverse))
        span *= 2
    return inverse


def invert_kernel(factor_ref, out_ref):
    panel, width = factor_ref.shape
    out_ref[...] = factor_ref[...]
    start = lax.axis_index("row") * panel - lax.axis_index("col") * width
    for offset in range(0, width, panel):

        @pl.when(start == offset)
        def _():
            for sub in range(0, panel, SUB):
                here = slice(sub, sub + SUB)
                there = slice(offset + sub, offset + sub + SUB)
                out_ref[here, there] = invert_lower(factor_ref[here, there])


def greet(peers):
    barrier = pltpu.get_barrier_semaphore()
    me = lax.axis_index("row")
    for step in range(1, peers):
        pl.semaphore_signal(
            barrier, inc=1, device_id={"row": lax.rem(me + step, peers)}, device_id_type=MESH
        )
    pl.semaphore_wait(barrier, peers - 1)


def scatter_kernel(peers, block_ref, out_ref, send_sem, recv_sem, own_sem):
    me = lax.axis_index("row")
    panel = block_ref.shape[0]
    width = out_ref.shape[1]
    greet(peers)

    def piece(peer, owner):
        return pltpu.make_async_remote_copy(
            src_ref=block_ref.at[:, pl.ds(pl.multiple_of(peer * width, LANES), width)],
            dst_ref=out_ref.at[pl.ds(pl.multiple_of(owner * panel, panel), panel), :],
            send_sem=send_sem.at[peer],
            recv_sem=recv_sem.at[owner],
            device_id={"row": peer},
            device_id_type=MESH,
        )

    for step in range(1, peers):
        piece(lax.rem(me + step, peers), me).start()
    own = pltpu.make_async_copy(
        block_ref.at[:, pl.ds(pl.multiple_of(me * width, LANES), width)],
        out_ref.at[pl.ds(pl.multiple_of(me * panel, panel), panel), :],
        own_sem,
    )
    own.start()
    own.wait()
    for step in range(1, peers):
        piece(lax.rem(me + step, peers), me).wait_send()
    for step in range(1, peers):
        owner = lax.rem(me + step, peers)
        piece(owner, owner).wait_recv()


def solve_kernel(
    peers, cols, work_ref, factor_ref, out_ref, solved, high, low, total, send_sem, recv_sem, own_sem
):
    me = lax.axis_index("row")
    panel, span = factor_ref.shape[1:]
    width = work_ref.shape[1]
    panels = cols * span // panel
    here = pl.ds(pl.multiple_of(me * width, LANES), width)
    greet(peers)

    def piece(target, owner):
        return pltpu.make_async_remote_copy(
            src_ref=solved.at[pl.ds(pl.multiple_of(target * panel, panel), panel), :],
            dst_ref=out_ref.at[:, pl.ds(pl.multiple_of(owner * width, LANES), width)],
            send_sem=send_sem.at[target],
            recv_sem=recv_sem.at[owner],
            device_id={"row": target},
            device_id_type=MESH,
        )

    for k in range(peers):
        rows = slice(k * panel, (k + 1) * panel)
        full = min(k * panel // span, cols)
        total[...] = work_ref[rows, :]
        if full:

            @pl.loop(0, full)
            def _(c):
                part = pl.ds(pl.multiple_of(c * span, span), span)
                total[...] -= dot3(factor_ref[k * cols + c], high[part, :], low[part, :])

        if k < panels:
            c, offset = full, k * panel - full * span
            if offset:
                part = slice(c * span, c * span + offset)
                total[...] -= dot3(
                    factor_ref[k * cols + c, :, 0:offset], high[part, :], low[part, :]
                )
            for sub in range(0, panel, SUB):
                value = total[sub : sub + SUB, :]
                if sub:
                    part = slice(k * panel, k * panel + sub)
                    value = value - dot3(
                        factor_ref[k * cols + c, sub : sub + SUB, offset : offset + sub],
                        high[part, :],
                        low[part, :],
                    )
                inverse = factor_ref[
                    k * cols + c, sub : sub + SUB, offset + sub : offset + sub + SUB
                ]
                value = dot3(inverse, *split(value))
                part = slice(k * panel + sub, k * panel + sub + SUB)
                solved[part, :] = value
                high[part, :], low[part, :] = split(value)
        else:
            solved[rows, :] = total[...]

        @pl.when(me != k)
        def _():
            piece(k, me).start()

        @pl.when(me == k)
        def _():
            pltpu.make_async_copy(solved.at[rows, :], out_ref.at[:, here], own_sem).start()

    pltpu.make_async_copy(solved.at[0:panel, :], out_ref.at[:, here], own_sem).wait()
    for step in range(1, peers):
        other = lax.rem(me + step, peers)
        piece(other, me).wait_send()
    for step in range(1, peers):
        other = lax.rem(me + step, peers)
        piece(other, other).wait_recv()


def shards(peers, cols, integrals, factor):
    panel, columns = integrals.shape
    span = factor.shape[1]
    width = -(-columns // (peers * LANES)) * LANES
    rows = peers * panel
    anywhere = pl.BlockSpec(memory_space=pl.ANY)
    vmem = pl.BlockSpec(memory_space=pltpu.VMEM)

    ready = pl.pallas_call(
        invert_kernel,
        out_shape=jax.ShapeDtypeStruct(factor.shape, jnp.float32),
        in_specs=[vmem],
        out_specs=vmem,
    )(factor)
    whole = lax.all_gather(ready, ("row", "col"))

    padded = jnp.pad(integrals, ((0, 0), (0, width * peers - columns)))
    work = pl.pallas_call(
        functools.partial(scatter_kernel, peers),
        out_shape=jax.ShapeDtypeStruct((rows, width), jnp.float32),
        in_specs=[anywhere],
        out_specs=anywhere,
        scratch_shapes=[
            pltpu.SemaphoreType.DMA((peers,)),
            pltpu.SemaphoreType.DMA((peers,)),
            pltpu.SemaphoreType.DMA,
        ],
        compiler_params=pltpu.CompilerParams(collective_id=0, has_side_effects=True),
        cost_estimate=pl.CostEstimate(
            flops=0, bytes_accessed=40 * rows * width * 4, transcendentals=0
        ),
    )(padded)

    out = pl.pallas_call(
        functools.partial(solve_kernel, peers, cols),
        out_shape=jax.ShapeDtypeStruct((panel, width * peers), jnp.float32),
        in_specs=[vmem, vmem],
        out_specs=anywhere,
        scratch_shapes=[
            pltpu.VMEM((rows, width), jnp.float32),
            pltpu.VMEM((cols * span, width), jnp.bfloat16),
            pltpu.VMEM((cols * span, width), jnp.bfloat16),
            pltpu.VMEM((panel, width), jnp.float32),
            pltpu.SemaphoreType.DMA((peers,)),
            pltpu.SemaphoreType.DMA((peers,)),
            pltpu.SemaphoreType.DMA,
        ],
        compiler_params=pltpu.CompilerParams(
            collective_id=1, has_side_effects=True, vmem_limit_bytes=60 * 1024 * 1024
        ),
        cost_estimate=pl.CostEstimate(
            flops=rows * cols * span * width * 3, bytes_accessed=rows * width * 8, transcendentals=0
        ),
    )(work, whole)
    return out[:, :columns]


def solution(mesh):
    placed = (P("row", "col"), P("row", "col"))
    body = functools.partial(shards, mesh.shape["row"], mesh.shape["col"])
    return jax.shard_map(
        body, mesh=mesh, in_specs=placed, out_specs=P("row", "col"), check_vma=False
    )
```

time: 1730 us -> 360 us (0.21)
  waiting for transfers between devices: 1320 us -> 25.5 us
  Pallas kernels: 0 us -> 314 us
  other arithmetic: 185 us -> 0 us
  matrix products: 165 us -> 0 us
  local copies, waits for them, and re-layouts: 36 us -> 5.41 us
    psum x8 -> x0, waiting for transfers between devices: 1290 us -> none  [spread(): return lax.psum(kept, axis)]
    pallas_call x0 -> x3, Pallas kernels: none -> 314 us  [the longest x1 176 us: shards(): pl.pallas_call(functools.partial(scatter_kernel, peers), out_shape=jax.Sh...]
    another operation x10 -> x0, other arithmetic: 162 us -> none  [local_solve(): return jax.scipy.linalg.solve_triangular(lower_block, current, lower=True)]
    dot_general x8 -> x0, matrix products: 102 us -> none  [apply_panel(): jnp.dot(factor_block, solved, precision=lax.Precision.HIGHEST, preferred_...]
    another operation x24 -> x0, matrix products: 62.8 us -> none  [local_solve(): return jax.scipy.linalg.solve_triangular(lower_block, current, lower=True)]
    another operation x57 -> x0, local copies, waits for them, and re-layouts: 35.9 us -> none  [local_solve(): return jax.scipy.linalg.solve_triangular(lower_block, current, lower=True)]
    select_n x8 -> x0, other arithmetic: 23.3 us -> none  [spread(): jnp.where(lax.axis_index(axis) == source, value, 0).astype(value.dtype)]
  transfers between devices with their start and end apart: 9 -> 1, of which waited for: 9 -> 1; matrix products, arithmetic and copies ran while one was open for 10% -> 0% of each run, Pallas kernels for 0% -> 49%
where the time goes in v1:
time: 360 us; the launch traced here: 358 us
  Pallas kernels  314 us (87%)
  waiting for transfers between devices  25.5 us (7%)
  between operations  13.4 us (4%)
  local copies, waits for them, and re-layouts  5.41 us (2%)
    pallas_call x1, Pallas kernels, shards(): pl.pallas_call(functools.partial(scatter_kernel, peers), out_shape=jax.Sh...  176 us
    pallas_call x1, Pallas kernels, shards(): pl.pallas_call(functools.partial(solve_kernel, peers, cols), out_shape=ja...  136 us
    all_gather x1, waiting for transfers between devices, shards(): whole = lax.all_gather(ready, ('row', 'col'))  25.5 us
  transfers between devices with their start and end apart: 1, of which 1 were waited for; matrix products, arithmetic and copies ran while one was open for 0% of the time, Pallas kernels for 49%

profile of v1, /device:TPU:28, one launch (start us, length us, event | category | flops | bytes accessed | tf_op | source)
XLA Modules:
  0.0 358.3 jit_solution(3403748117939460709)
XLA Ops:
  6.5 0.0 all-gather.3.cloned.1.call-start
  6.5 2.0 shard_map.29
  8.6 0.0 all-gather.3.cloned.1.call-update
  8.6 175.8 %shard_map.28.work_ref = f32[2048,640]{1,0:T(8,128)} custom-call(f32[256,5120]{1,0:T(8,128)} %block_ref.1), custom_call_target="tpu_custom_call" | custom-call | bytes 209715200 | tf_op jit(solution)/shard_map/pallas_call | solution.py:190
  184.5 25.5 %all-gather.3.cloned.1.call-done = f32[8192,512]{1,0:T(8,128)} async-done(((f32[256,512]{1,0:T(8,128)}), f32[8192,512]{1,0:T(8,128)}) %all-gather.3.cloned.1.call-update) | async-done | bytes 16777232 | tf_op jit(solution)/shard_map/all_gather | solution.py:187
  210.0 136.0 %shard_map.30 = f32[256,5120]{1,0:T(8,128)} custom-call(f32[2048,640]{1,0:T(8,128)} %shard_map.28.work_ref, f32[32,256,512]{2,1,0:T(8,128)} %bitcast.1), custom_call_target="tpu_custom_call" | custom-call | flops 8053063680 | bytes 10485760 | tf_op jit(solution)/shard_map/pallas_call | solution.py:206
  346.0 5.4 %copy.4 = f32[256,5120]{1,0:T(8,128)} copy(f32[256,5120]{1,0:T(8,128)} %shard_map.30) | data formatting | bytes 10485760
Async XLA Ops:
  6.5 203.5 %all-gather.3.cloned.1.call-start = ((), (), s32[]{:S(2)}) async-start(), calls=%async_computation | async-start | bytes 17301504 | tf_op jit(solution)/shard_map/all_gather | solution.py:187
Sparse Core Ops, SparseCore 0:
  10.2 199.7 all-gather.2

commit v2 on v1

v2 whole, which is shorter than its diff:
```python
import functools

import jax
import jax.numpy as jnp
from jax import lax
from jax.experimental import pallas as pl
from jax.experimental.pallas import tpu as pltpu
from jax.sharding import PartitionSpec as P

MESH = pl.DeviceIdType.MESH
SUB = 128
LANES = 128


def split(value):
    high = value.astype(jnp.bfloat16)
    return high, (value - high.astype(jnp.float32)).astype(jnp.bfloat16)


def dot3(left, right_high, right_low):
    left_high, left_low = split(left)
    mm = functools.partial(jnp.dot, preferred_element_type=jnp.float32)
    return mm(left_high, right_high) + (mm(left_high, right_low) + mm(left_low, right_high))


def invert_lower(block):
    size = block.shape[0]
    mm = functools.partial(
        jnp.dot, precision=lax.Precision.HIGHEST, preferred_element_type=jnp.float32
    )
    rows = lax.broadcasted_iota(jnp.int32, (size, size), 0)
    cols = lax.broadcasted_iota(jnp.int32, (size, size), 1)
    inverse = jnp.where(rows == cols, 1.0 / jnp.where(rows == cols, block, 1.0), 0.0)
    span = 1
    while span < size:
        pair = (rows // (2 * span) == cols // (2 * span)) & (rows // span > cols // span)
        below = jnp.where(pair, block, 0.0)
        inverse = inverse - mm(inverse, mm(below, inverse))
        span *= 2
    return inverse


def kernel(
    peers,
    cols,
    block_ref,
    factor_ref,
    out_ref,
    work,
    whole,
    solved,
    high,
    low,
    total,
    own_sem,
    there_send,
    there_recv,
    back_send,
    back_recv,
    whole_recv,
    far_send,
    near_send,
    across_send,
    core_send,
):
    me, col = lax.axis_index("row"), lax.axis_index("col")
    panel, span = factor_ref.shape
    width = work.shape[1]
    panels = cols * span // panel
    groups, chips = peers // 2, cols // 2
    group, side = me // 2, lax.rem(me, 2)
    chip, core = col // 2, lax.rem(col, 2)

    def far(step):
        return lax.rem(group + step, groups) * 2

    def across(step):
        return lax.rem(chip + step, chips) * 2 + core

    other_side = {"row": group * 2 + 1 - side}
    other_core = {"col": chip * 2 + 1 - core}

    barrier = pltpu.get_barrier_semaphore()
    friends = [{"row": lax.rem(me + step, peers)} for step in range(1, peers)]
    friends += [{"col": across(step)} for step in range(1, chips)] + [other_core]
    for friend in friends:
        pl.semaphore_signal(barrier, inc=1, device_id=friend, device_id_type=MESH)
    pl.semaphore_wait(barrier, len(friends))

    def rows_of(peer):
        return pl.ds(pl.multiple_of(peer * panel, panel), panel)

    def columns_of(peer):
        return pl.ds(pl.multiple_of(peer * width, LANES), width)

    def send_work(peer, owner):
        return pltpu.make_async_remote_copy(
            src_ref=block_ref.at[:, columns_of(peer)],
            dst_ref=work.at[rows_of(owner), :],
            send_sem=there_send.at[peer],
            recv_sem=there_recv.at[owner],
            device_id={"row": peer},
            device_id_type=MESH,
        )

    def send_solved(target, owner):
        return pltpu.make_async_remote_copy(
            src_ref=solved.at[rows_of(target), :],
            dst_ref=out_ref.at[:, columns_of(owner)],
            send_sem=back_send.at[target],
            recv_sem=back_recv.at[owner],
            device_id={"row": target},
            device_id_type=MESH,
        )

    def send_factor(row, column, sem, device):
        index = row * cols + column
        return pltpu.make_async_remote_copy(
            src_ref=whole.at[index],
            dst_ref=whole.at[index],
            send_sem=sem,
            recv_sem=whole_recv.at[index],
            device_id=device,
            device_id_type=MESH,
        )

    def needed(row, column):
        return column * span < (row + 1) * panel

    def arrived(row, column):
        send_factor(row, column, core_send.at[0], other_core).wait_recv()

    def copies(row, column, own, near, chip_step):
        found = []
        index = row * chips + column // 2
        if own:
            for step in range(1, groups):
                found.append(
                    send_factor(row, column, far_send.at[step], {"row": far(step) + side})
                )
        if near:
            found.append(send_factor(row, column, near_send.at[row // 2], other_side))
        if chip_step == 0:
            for step in range(1, chips):
                sem = across_send.at[row * chips + step]
                found.append(send_factor(row, column, sem, {"col": across(step)}))
        found.append(send_factor(row, column, core_send.at[index], other_core))
        return found

    relayed = [(me, col, True, True, 0)]
    relayed += [(far(step) + side, col, False, True, 0) for step in range(1, groups)]
    relayed += [(far(step) + 1 - side, col, False, False, 0) for step in range(groups)]
    for step in range(1, chips):
        relayed += [(row, across(step), False, False, step) for row in range(peers)]

    for step in range(1, peers):
        send_work(lax.rem(me + step, peers), me).start()
    own = pltpu.make_async_copy(
        block_ref.at[:, columns_of(me)], work.at[rows_of(me), :], own_sem
    )
    own.start()

    mine = me * cols + col
    whole[mine] = factor_ref[...]
    start = me * panel - col * span
    for offset in range(0, span, panel):

        @pl.when(start == offset)
        def _():
            for sub in range(0, panel, SUB):
                there = slice(offset + sub, offset + sub + SUB)
                whole[mine, sub : sub + SUB, there] = invert_lower(
                    factor_ref[sub : sub + SUB, there]
                )

    for row, column, is_own, near, chip_step in relayed:

        @pl.when(needed(row, column))
        def _():
            if not is_own:
                arrived(row, column)
            for copy in copies(row, column, is_own, near, chip_step):
                copy.start()

    own.wait()

    for k in range(peers):
        rows = slice(k * panel, (k + 1) * panel)
        full = min(k * panel // span, cols)

        @pl.when(me != k)
        def _():
            send_work(k, k).wait_recv()

        for step in range(chips):
            column = step * 2 + 1 - core

            @pl.when(needed(k, column))
            def _():
                arrived(k, column)

        total[...] = work[rows, :]
        if full:

            @pl.loop(0, full)
            def _(c):
                part = pl.ds(pl.multiple_of(c * span, span), span)
                total[...] -= dot3(whole[k * cols + c], high[part, :], low[part, :])

        if k < panels:
            c, offset = full, k * panel - full * span
            if offset:
                part = slice(c * span, c * span + offset)
                total[...] -= dot3(whole[k * cols + c, :, 0:offset], high[part, :], low[part, :])
            for sub in range(0, panel, SUB):
                value = total[sub : sub + SUB, :]
                if sub:
                    part = slice(k * panel, k * panel + sub)
                    value = value - dot3(
                        whole[k * cols + c, sub : sub + SUB, offset : offset + sub],
                        high[part, :],
                        low[part, :],
                    )
                inverse = whole[k * cols + c, sub : sub + SUB, offset + sub : offset + sub + SUB]
                value = dot3(inverse, *split(value))
                part = slice(k * panel + sub, k * panel + sub + SUB)
                solved[part, :] = value
                high[part, :], low[part, :] = split(value)
        else:
            solved[rows, :] = total[...]

        @pl.when(me != k)
        def _():
            send_solved(k, me).start()

        @pl.when(me == k)
        def _():
            pltpu.make_async_copy(solved.at[rows, :], out_ref.at[:, columns_of(me)], own_sem).start()

    pltpu.make_async_copy(solved.at[0:panel, :], out_ref.at[:, columns_of(me)], own_sem).wait()
    for row, column, is_own, near, chip_step in relayed:

        @pl.when(needed(row, column))
        def _():
            for copy in copies(row, column, is_own, near, chip_step):
                copy.wait_send()

    for step in range(1, peers):
        other = lax.rem(me + step, peers)
        send_work(other, me).wait_send()
        send_solved(other, me).wait_send()
    for step in range(1, peers):
        other = lax.rem(me + step, peers)
        send_solved(other, other).wait_recv()


def shards(peers, cols, integrals, factor):
    panel, columns = integrals.shape
    span = factor.shape[1]
    width = -(-columns // (peers * LANES)) * LANES
    rows = peers * panel
    anywhere = pl.BlockSpec(memory_space=pl.ANY)
    padded = jnp.pad(integrals, ((0, 0), (0, width * peers - columns)))
    dma = pltpu.SemaphoreType.DMA
    out = pl.pallas_call(
        functools.partial(kernel, peers, cols),
        out_shape=jax.ShapeDtypeStruct((panel, width * peers), jnp.float32),
        in_specs=[anywhere, pl.BlockSpec(memory_space=pltpu.VMEM)],
        out_specs=anywhere,
        scratch_shapes=[
            pltpu.VMEM((rows, width), jnp.float32),
            pltpu.VMEM((peers * cols, panel, span), jnp.float32),
            pltpu.VMEM((rows, width), jnp.float32),
            pltpu.VMEM((cols * span, width), jnp.bfloat16),
            pltpu.VMEM((cols * span, width), jnp.bfloat16),
            pltpu.VMEM((panel, width), jnp.float32),
            dma,
            dma((peers,)),
            dma((peers,)),
            dma((peers,)),
            dma((peers,)),
            dma((peers * cols,)),
            dma((peers // 2,)),
            dma((peers // 2,)),
            dma((peers * cols // 2,)),
            dma((peers * cols // 2,)),
        ],
        compiler_params=pltpu.CompilerParams(
            collective_id=0, has_side_effects=True, vmem_limit_bytes=60 * 1024 * 1024
        ),
        cost_estimate=pl.CostEstimate(
            flops=rows * cols * span * width * 3, bytes_accessed=rows * width * 8, transcendentals=0
        ),
    )(padded, factor)
    return out[:, :columns]


def solution(mesh):
    placed = (P("row", "col"), P("row", "col"))
    body = functools.partial(shards, mesh.shape["row"], mesh.shape["col"])
    return jax.shard_map(
        body, mesh=mesh, in_specs=placed, out_specs=P("row", "col"), check_vma=False
    )
```

time: 360 us -> 360 us (level)
  the two profiles are of different devices: /device:TPU:28 before, /device:TPU:31 now
where the time goes in v2:
time: 360 us; the launch traced here: 359 us
  Pallas kernels  354 us (98%)
  local copies, waits for them, and re-layouts  5.41 us (2%)
    pallas_call x1, Pallas kernels, shards(): pl.pallas_call(functools.partial(kernel, peers, cols), out_shape=jax.Shap...  354 us

profile of v2, /device:TPU:31, one launch (start us, length us, event | category | flops | bytes accessed | tf_op | source)
XLA Modules:
  0.0 359.4 jit_solution(13798145984892923857)
XLA Ops:
  0.0 354.0 %shard_map.28 = f32[256,5120]{1,0:T(8,128)} custom-call(f32[256,5120]{1,0:T(8,128)} %block_ref.1, f32[256,512]{1,0:T(8,128)} %factor_ref.1), custom_call_target="tpu_custom_call" | custom-call | flops 8053063680 | bytes 10485760 | tf_op jit(solution)/shard_map/pallas_call | solution.py:265
  354.0 5.4 %copy.4 = f32[256,5120]{1,0:T(8,128)} copy(f32[256,5120]{1,0:T(8,128)} %shard_map.28) | data formatting | bytes 10485760

commit v3 on v2

--- a/solution.py
+++ b/solution.py
@@ -10,6 +10,7 @@
 MESH = pl.DeviceIdType.MESH
 SUB = 128
 LANES = 128
+AHEAD = 2
 
 
 def split(value):
@@ -153,8 +154,6 @@
     for step in range(1, chips):
         relayed += [(row, across(step), False, False, step) for row in range(peers)]
 
-    for step in range(1, peers):
-        send_work(lax.rem(me + step, peers), me).start()
     own = pltpu.make_async_copy(
         block_ref.at[:, columns_of(me)], work.at[rows_of(me), :], own_sem
     )
@@ -173,6 +172,7 @@
                     factor_ref[sub : sub + SUB, there]
                 )
 
+    waiting = list(range(1, peers))
     for row, column, is_own, near, chip_step in relayed:
 
         @pl.when(needed(row, column))
@@ -182,6 +182,12 @@
             for copy in copies(row, column, is_own, near, chip_step):
                 copy.start()
 
+        for _ in range(AHEAD if is_own else 1):
+            if waiting:
+                send_work(lax.rem(me + waiting.pop(0), peers), me).start()
+
+    for step in waiting:
+        send_work(lax.rem(me + step, peers), me).start()
     own.wait()
 
     for k in range(peers):

time: 360 us -> 345 us (0.958)
  the two profiles are of different devices: /device:TPU:31 before, /device:TPU:28 now
where the time goes in v3:
time: 345 us
  Pallas kernels  340 us (99%)
  local copies, waits for them, and re-layouts  5.41 us (2%)
    pallas_call x1, Pallas kernels, shards(): pl.pallas_call(functools.partial(kernel, peers, cols), out_shape=jax.Shap...  340 us

profile of v3, /device:TPU:28, one launch (start us, length us, event | category | flops | bytes accessed | tf_op | source)
XLA Modules:
  0.0 345.2 jit_solution(14945278625687572279)
XLA Ops:
  0.0 339.8 %shard_map.28 = f32[256,5120]{1,0:T(8,128)} custom-call(f32[256,5120]{1,0:T(8,128)} %block_ref.1, f32[256,512]{1,0:T(8,128)} %factor_ref.1), custom_call_target="tpu_custom_call" | custom-call | flops 8053063680 | bytes 10485760 | tf_op jit(solution)/shard_map/pallas_call | solution.py:271
  339.8 5.4 %copy.4 = f32[256,5120]{1,0:T(8,128)} copy(f32[256,5120]{1,0:T(8,128)} %shard_map.28) | data formatting | bytes 10485760

commit v4 on v3

--- a/solution.py
+++ b/solution.py
@@ -10,7 +10,7 @@
 MESH = pl.DeviceIdType.MESH
 SUB = 128
 LANES = 128
-AHEAD = 2
+AHEAD = 4
 
 
 def split(value):

time: 345 us -> 345 us (level)
  no operation moved by 1% of the time
where the time goes in v4:
time: 345 us
  Pallas kernels  339 us (98%)
  local copies, waits for them, and re-layouts  5.41 us (2%)
    pallas_call x1, Pallas kernels, shards(): pl.pallas_call(functools.partial(kernel, peers, cols), out_shape=jax.Shap...  339 us

profile of v4, /device:TPU:28, one launch (start us, length us, event | category | flops | bytes accessed | tf_op | source)
XLA Modules:
  0.0 344.8 jit_solution(15354468373956765966)
XLA Ops:
  0.0 339.4 %shard_map.28 = f32[256,5120]{1,0:T(8,128)} custom-call(f32[256,5120]{1,0:T(8,128)} %block_ref.1, f32[256,512]{1,0:T(8,128)} %factor_ref.1), custom_call_target="tpu_custom_call" | custom-call | flops 8053063680 | bytes 10485760 | tf_op jit(solution)/shard_map/pallas_call | solution.py:271
  339.4 5.4 %copy.4 = f32[256,5120]{1,0:T(8,128)} copy(f32[256,5120]{1,0:T(8,128)} %shard_map.28) | data formatting | bytes 10485760

commit v5 on v3

--- a/solution.py
+++ b/solution.py
@@ -172,7 +172,7 @@
                     factor_ref[sub : sub + SUB, there]
                 )
 
-    waiting = list(range(1, peers))
+    waiting = sorted(range(1, peers), key=lambda step: abs(2 * step - peers))
     for row, column, is_own, near, chip_step in relayed:
 
         @pl.when(needed(row, column))

time: 345 us -> 348 us (level)
  no operation moved by 1% of the time
where the time goes in v5:
time: 348 us; the launch traced here: 347 us
  Pallas kernels  342 us (98%)
  local copies, waits for them, and re-layouts  5.41 us (2%)
    pallas_call x1, Pallas kernels, shards(): pl.pallas_call(functools.partial(kernel, peers, cols), out_shape=jax.Shap...  342 us

profile of v5, /device:TPU:28, one launch (start us, length us, event | category | flops | bytes accessed | tf_op | source)
XLA Modules:
  0.0 347.4 jit_solution(10919283540940656236)
XLA Ops:
  0.0 341.9 %shard_map.28 = f32[256,5120]{1,0:T(8,128)} custom-call(f32[256,5120]{1,0:T(8,128)} %block_ref.1, f32[256,512]{1,0:T(8,128)} %factor_ref.1), custom_call_target="tpu_custom_call" | custom-call | flops 8053063680 | bytes 10485760 | tf_op jit(solution)/shard_map/pallas_call | solution.py:271
  341.9 5.4 %copy.4 = f32[256,5120]{1,0:T(8,128)} copy(f32[256,5120]{1,0:T(8,128)} %shard_map.28) | data formatting | bytes 10485760
